TPU v7x, 32 devices: a whole 2x2x4 slice. The times are simulated.
32 devices in a mesh: dp: 8 (over y, x, core), fsdp: 4 (over z).
Axes of the slice: x: 2, y: 2, z: 4, core: 2. Of those that a mesh axis runs over, the one named last changes fastest.
Arguments:
- hidden_in: bfloat16 [16384, 768], P(('dp', 'fsdp')), may hold values from -6 to 6
- lengths: int32 [1024], P(('dp', 'fsdp')), may hold values from 4 to 16
- images: bfloat16 [1024, 768], P(('dp', 'fsdp')), may hold values from -12 to 12
- labels: int32 [1024], P(('dp', 'fsdp')), may hold values from 0 to 1023, each once
- wide_master: float32 [768, 6144], P('fsdp'), may hold values from -0.18042196 to 0.18042196
- down_master: float32 [3072, 768], P('fsdp'), may hold values from -0.109375 to 0.109375
- vector_master: float32 [12, 768], P(None, 'fsdp'), may hold values from -0.5 to 1.5
- wide_momentum: float32 [768, 6144], P('fsdp'), may hold values from -7.68 to 7.68
- down_momentum: float32 [3072, 768], P('fsdp'), may hold values from -7.68 to 7.68
- vector_momentum: float32 [12, 768], P(None, 'fsdp'), may hold values from -38.4 to 38.4
- wide_average: float32 [768, 6144], P('fsdp'), may hold values from -0.18042196 to 0.18042196
- down_average: float32 [3072, 768], P('fsdp'), may hold values from -0.109375 to 0.109375
- vector_average: float32 [12, 768], P(None, 'fsdp'), may hold values from -0.5 to 1.5
Outputs:
- block_out: bfloat16 [16384, 768], P(('dp', 'fsdp'))
- input_grad: float32 [16384, 768], P(('dp', 'fsdp'))
- wide_new: float32 [768, 6144], P('fsdp')
- down_new: float32 [3072, 768], P('fsdp')
- vector_new: float32 [12, 768], P(None, 'fsdp')
- wide_momentum_new: float32 [768, 6144], P('fsdp')
- down_momentum_new: float32 [3072, 768], P('fsdp')
- vector_momentum_new: float32 [12, 768], P(None, 'fsdp')
- wide_average_new: float32 [768, 6144], P('fsdp')
- down_average_new: float32 [3072, 768], P('fsdp')
- vector_average_new: float32 [12, 768], P(None, 'fsdp')
- wide_copy: bfloat16 [768, 6144], P('fsdp')
- down_copy: bfloat16 [3072, 768], P('fsdp')
- vector_copy: bfloat16 [12, 768], P(None, 'fsdp')
Inputs may be any that keep to these rules, and one draw needn't show every extreme that they name: labels name every caption exactly once.
All inputs are finite; a program needn't handle non-finite values.
Results may differ from a plain program's by a relative error of at most 0.017.
Values may be sent and summed in bfloat16 or wider, within the bound.
No kernel may reach another device: no remote copies, remote signals or barrier semaphores. Data moves between devices by JAX's collectives and lax.ppermute only.
A program may use at most 192 MiB of HBM per device.

v0:
```python
import jax
import jax.numpy as jnp
from jax import lax
from jax.sharding import PartitionSpec as P

HEADS = 12
SEQ = 16
MICRO = 2


norm_epsilon = 1e-06
masked_score = -1e30
learn_rate = 0.02
momentum_decay = 0.5
average_decay = 0.5
contract_rows = (((0,), (0,)), ((), ()))
contract_cols = (((1,), (1,)), ((), ()))


def layer_norm(values, scale_row, shift_row):
    centre = values - jnp.mean(values, axis=-1, keepdims=True)
    spread = jnp.mean(centre * centre, axis=-1, keepdims=True)
    return centre * lax.rsqrt(spread + norm_epsilon) * scale_row + shift_row


def forward(token_rows, seq_lens, weights):
    wide_w, down_w, vectors = weights
    vec_f = vectors.astype(jnp.float32)
    model_width = token_rows.shape[1]
    captions = seq_lens.shape[0]
    seq_len = token_rows.shape[0] // captions
    head_size = model_width // HEADS
    token_x = token_rows.astype(jnp.float32)
    normed = layer_norm(token_x, vec_f[0], vec_f[1]).astype(jnp.bfloat16)
    qkv_bias = jnp.concatenate([vec_f[2], jnp.zeros_like(vec_f[2]), vec_f[3]])
    joined = (
        jnp.dot(normed, wide_w[:, : 3 * model_width], preferred_element_type=jnp.float32) + qkv_bias
    ).astype(jnp.bfloat16)
    queries = joined[:, :model_width].reshape(captions, seq_len, HEADS, head_size)
    key_heads = joined[:, model_width : 2 * model_width].reshape(
        captions, seq_len, HEADS, head_size
    )
    value_heads = joined[:, 2 * model_width :].reshape(captions, seq_len, HEADS, head_size)
    key_mask = jnp.arange(seq_len)[None, :] < seq_lens[:, None]
    scores = jnp.einsum(
        "cqhd,ckhd->chqk", queries, key_heads, preferred_element_type=jnp.float32
    ) * head_size ** (-0.5)
    scores = jnp.where(key_mask[:, None, None, :], scores, masked_score)
    totals = jax.nn.logsumexp(scores, axis=-1, keepdims=True)
    attn_probs = jnp.exp(scores - totals)
    context = jnp.einsum(
        "chqk,ckhd->cqhd",
        attn_probs.astype(jnp.bfloat16),
        value_heads,
        preferred_element_type=jnp.float32,
    )
    context = context.reshape(captions * seq_len, model_width).astype(jnp.bfloat16)
    residual = token_x + (
        jnp.dot(
            context,
            wide_w[:, 3 * model_width : 4 * model_width],
            preferred_element_type=jnp.float32,
        )
        + vec_f[4]
    )
    second = layer_norm(residual, vec_f[5], vec_f[6]).astype(jnp.bfloat16)
    up_proj = jnp.dot(
        second, wide_w[:, 4 * model_width :], preferred_element_type=jnp.float32
    ) + vec_f[8:].reshape(-1)
    gelu_out = jax.nn.gelu(up_proj).astype(jnp.bfloat16)
    block_rows = residual + (
        jnp.dot(gelu_out, down_w, preferred_element_type=jnp.float32) + vec_f[7]
    )
    mask_f = key_mask.astype(jnp.float32)
    pooled = jnp.sum(
        block_rows.reshape(captions, seq_len, model_width) * mask_f[:, :, None], axis=1
    ) / seq_lens[:, None].astype(jnp.float32)
    inv_norm = lax.rsqrt(jnp.sum(pooled * pooled, axis=-1, keepdims=True) + norm_epsilon)
    text_emb = (pooled * inv_norm).astype(jnp.bfloat16)
    stored = (
        token_x,
        normed,
        queries,
        key_heads,
        value_heads,
        totals,
        context,
        residual,
        second,
        up_proj,
        gelu_out,
        pooled,
        inv_norm,
        key_mask,
    )
    return (block_rows, text_emb, stored)


def backward(text_grad, stored, weights, seq_lens):
    wide_w, down_w, vectors = weights
    vec_f = vectors.astype(jnp.float32)
    (
        token_x,
        normed,
        queries,
        key_heads,
        value_heads,
        totals,
        context,
        residual,
        second,
        up_proj,
        gelu_out,
        pooled,
        inv_norm,
        key_mask,
    ) = stored
    model_width = token_x.shape[1]
    captions = seq_lens.shape[0]
    seq_len = token_x.shape[0] // captions
    head_size = model_width // HEADS
    row_total = captions * seq_len
    d_pooled = inv_norm * text_grad - inv_norm**3 * pooled * jnp.sum(
        pooled * text_grad, axis=-1, keepdims=True
    )
    mask_f = key_mask.astype(jnp.float32)
    d_out = (
        (d_pooled / seq_lens[:, None].astype(jnp.float32))[:, None, :] * mask_f[:, :, None]
    ).reshape(row_total, model_width)
    d_branch = d_out.astype(jnp.bfloat16)
    g_down = lax.dot_general(gelu_out, d_branch, contract_rows, preferred_element_type=jnp.float32)
    g_down_bias = jnp.sum(d_branch.astype(jnp.float32), axis=0)
    d_gelu = lax.dot_general(d_branch, down_w, contract_cols, preferred_element_type=jnp.float32)
    d_up = jax.vjp(jax.nn.gelu, up_proj)[1](d_gelu)[0].astype(jnp.bfloat16)
    g_fc1 = lax.dot_general(second, d_up, contract_rows, preferred_element_type=jnp.float32)
    g_fc1_bias = jnp.sum(d_up.astype(jnp.float32), axis=0)
    d_second = lax.dot_general(
        d_up, wide_w[:, 4 * model_width :], contract_cols, preferred_element_type=jnp.float32
    )
    d_norm_two, g_gain_two, g_shift_two = jax.vjp(layer_norm, residual, vec_f[5], vec_f[6])[1](
        d_second
    )
    d_residual = d_out + d_norm_two
    d_attn = d_residual.astype(jnp.bfloat16)
    g_out = lax.dot_general(context, d_attn, contract_rows, preferred_element_type=jnp.float32)
    g_out_bias = jnp.sum(d_attn.astype(jnp.float32), axis=0)
    d_context = lax.dot_general(
        d_attn,
        wide_w[:, 3 * model_width : 4 * model_width],
        contract_cols,
        preferred_element_type=jnp.float32,
    )
    d_context = d_context.astype(jnp.bfloat16).reshape(captions, seq_len, HEADS, head_size)
    score_scale = head_size ** (-0.5)
    scores = (
        jnp.einsum("cqhd,ckhd->chqk", queries, key_heads, preferred_element_type=jnp.float32)
        * score_scale
    )
    scores = jnp.where(key_mask[:, None, None, :], scores, masked_score)
    attn_probs = jnp.exp(scores - totals)
    d_probs = jnp.einsum(
        "cqhd,ckhd->chqk", d_context, value_heads, preferred_element_type=jnp.float32
    )
    d_scores = (
        attn_probs * (d_probs - jnp.sum(attn_probs * d_probs, axis=-1, keepdims=True))
    ).astype(jnp.bfloat16)
    d_queries = (
        jnp.einsum("chqk,ckhd->cqhd", d_scores, key_heads, preferred_element_type=jnp.float32)
        * score_scale
    )
    d_keys = (
        jnp.einsum("chqk,cqhd->ckhd", d_scores, queries, preferred_element_type=jnp.float32)
        * score_scale
    )
    d_values = jnp.einsum(
        "chqk,cqhd->ckhd",
        attn_probs.astype(jnp.bfloat16),
        d_context,
        preferred_element_type=jnp.float32,
    )
    d_joined = jnp.concatenate(
        [
            d_queries.reshape(row_total, model_width),
            d_keys.reshape(row_total, model_width),
            d_values.reshape(row_total, model_width),
        ],
        axis=1,
    ).astype(jnp.bfloat16)
    g_qkv = lax.dot_general(normed, d_joined, contract_rows, preferred_element_type=jnp.float32)
    g_query_bias = jnp.sum(d_joined[:, :model_width].astype(jnp.float32), axis=0)
    g_value_bias = jnp.sum(d_joined[:, 2 * model_width :].astype(jnp.float32), axis=0)
    d_normed = lax.dot_general(
        d_joined, wide_w[:, : 3 * model_width], contract_cols, preferred_element_type=jnp.float32
    )
    d_norm_one, g_gain_one, g_shift_one = jax.vjp(layer_norm, token_x, vec_f[0], vec_f[1])[1](
        d_normed
    )
    input_grad = d_residual + d_norm_one
    wide_grad = jnp.concatenate([g_qkv, g_out, g_fc1], axis=1)
    vector_grad = jnp.concatenate(
        [
            jnp.stack(
                [
                    g_gain_one,
                    g_shift_one,
                    g_query_bias,
                    g_value_bias,
                    g_out_bias,
                    g_gain_two,
                    g_shift_two,
                    g_down_bias,
                ]
            ),
            g_fc1_bias.reshape(-1, model_width),
        ],
        axis=0,
    )
    return (input_grad, wide_grad, g_down, vector_grad)


def renew_state(master, momentum, average, gradient):
    momentum_new = momentum_decay * momentum + gradient
    master_new = master - learn_rate * (gradient + momentum_decay * momentum_new)
    average_new = average_decay * average + (1.0 - average_decay) * master_new
    return (master_new, momentum_new, average_new, master_new.astype(jnp.bfloat16))


def body(
    hidden_in,
    lengths,
    images,
    labels,
    wide_master,
    down_master,
    vector_master,
    wide_momentum,
    down_momentum,
    vector_momentum,
    wide_average,
    down_average,
    vector_average,
):
    own_copies = (
        wide_master.astype(jnp.bfloat16),
        down_master.astype(jnp.bfloat16),
        vector_master.astype(jnp.bfloat16),
    )
    captions = lengths.shape[0]
    per_micro = captions // MICRO
    rows_micro = per_micro * SEQ
    stored_list = []
    block_list = []
    text_list = []
    weight_list = []
    for micro_index in range(MICRO):
        weights = (
            lax.all_gather(own_copies[0], "fsdp", axis=0, tiled=True),
            lax.all_gather(own_copies[1], "fsdp", axis=0, tiled=True),
            lax.all_gather(own_copies[2], "fsdp", axis=1, tiled=True),
        )
        token_rows = hidden_in[micro_index * rows_micro : (micro_index + 1) * rows_micro]
        seq_lens = lengths[micro_index * per_micro : (micro_index + 1) * per_micro]
        block_rows, text_emb, stored = forward(token_rows, seq_lens, weights)
        stored_list.append(stored)
        block_list.append(block_rows)
        text_list.append(text_emb)
        weight_list.append(weights)
    local_texts = jnp.concatenate(text_list, axis=0)
    all_texts = lax.all_gather(local_texts, ("dp", "fsdp"), axis=0, tiled=True)
    total_count = all_texts.shape[0]
    logits = lax.dot_general(images, all_texts, contract_cols, preferred_element_type=jnp.float32)
    totals = jax.nn.logsumexp(logits, axis=-1)
    onehot = (jnp.arange(total_count)[None, :] == labels[:, None]).astype(jnp.float32)
    slopes = (jnp.exp(logits - totals[:, None]) - onehot).astype(jnp.bfloat16)
    text_grad = lax.psum_scatter(
        lax.dot_general(slopes, images, contract_rows, preferred_element_type=jnp.float32),
        ("dp", "fsdp"),
        scatter_dimension=0,
        tiled=True,
    )
    input_list = []
    wide_sum = None
    down_sum = None
    vector_sum = None
    for micro_index in range(MICRO):
        weights = (
            lax.all_gather(own_copies[0], "fsdp", axis=0, tiled=True),
            lax.all_gather(own_copies[1], "fsdp", axis=0, tiled=True),
            lax.all_gather(own_copies[2], "fsdp", axis=1, tiled=True),
        )
        seq_lens = lengths[micro_index * per_micro : (micro_index + 1) * per_micro]
        grad_part = text_grad[micro_index * per_micro : (micro_index + 1) * per_micro]
        input_part, wide_part, down_part, vector_part = backward(
            grad_part, stored_list[micro_index], weights, seq_lens
        )
        input_list.append(input_part)
        if wide_sum is None:
            wide_sum, down_sum, vector_sum = (wide_part, down_part, vector_part)
        else:
            wide_sum = wide_sum + wide_part
            down_sum = down_sum + down_part
            vector_sum = vector_sum + vector_part
    shares = (
        lax.psum_scatter(
            wide_sum.astype(jnp.bfloat16), "fsdp", scatter_dimension=0, tiled=True
        ).astype(jnp.float32),
        lax.psum_scatter(
            down_sum.astype(jnp.bfloat16), "fsdp", scatter_dimension=0, tiled=True
        ).astype(jnp.float32),
        lax.psum_scatter(
            vector_sum.astype(jnp.bfloat16), "fsdp", scatter_dimension=1, tiled=True
        ).astype(jnp.float32),
    )
    reduced = (
        lax.psum(shares[0].astype(jnp.bfloat16), "dp").astype(jnp.float32),
        lax.psum(shares[1].astype(jnp.bfloat16), "dp").astype(jnp.float32),
        lax.psum(shares[2].astype(jnp.bfloat16), "dp").astype(jnp.float32),
    )
    wide_state = renew_state(wide_master, wide_momentum, wide_average, reduced[0])
    down_state = renew_state(down_master, down_momentum, down_average, reduced[1])
    vector_state = renew_state(vector_master, vector_momentum, vector_average, reduced[2])
    block_out = jnp.concatenate(block_list, axis=0).astype(jnp.bfloat16)
    input_grad = jnp.concatenate(input_list, axis=0)
    return (
        block_out,
        input_grad,
        wide_state[0],
        down_state[0],
        vector_state[0],
        wide_state[1],
        down_state[1],
        vector_state[1],
        wide_state[2],
        down_state[2],
        vector_state[2],
        wide_state[3],
        down_state[3],
        vector_state[3],
    )


def solution(mesh):
    return jax.shard_map(
        body,
        mesh=mesh,
        in_specs=(
            P(("dp", "fsdp"), None),
            P(("dp", "fsdp")),
            P(("dp", "fsdp"), None),
            P(("dp", "fsdp")),
            P("fsdp", None),
            P("fsdp", None),
            P(None, "fsdp"),
            P("fsdp", None),
            P("fsdp", None),
            P(None, "fsdp"),
            P("fsdp", None),
            P("fsdp", None),
            P(None, "fsdp"),
        ),
        out_specs=(
            P(("dp", "fsdp"), None),
            P(("dp", "fsdp"), None),
            P("fsdp", None),
            P("fsdp", None),
            P(None, "fsdp"),
            P("fsdp", None),
            P("fsdp", None),
            P(None, "fsdp"),
            P("fsdp", None),
            P("fsdp", None),
            P(None, "fsdp"),
            P("fsdp", None),
            P("fsdp", None),
            P(None, "fsdp"),
        ),
        check_vma=False,
    )
```

profile of v0, /device:TPU:0, one launch (start us, length us, event | category | flops | bytes accessed | tf_op | source)
XLA Modules:
  0.0 838.1 jit_solution(15479007363936414460)
XLA Ops:
  7.3 4.2 convert_element_type.229
  13.0 14.8 %all-gather = bf16[4,192,12]{1,2,0:T(8,128)(2,1)S(1)} all-gather(bf16[1,192,12]{1,2,0:T(8,128)(2,1)S(1)} %convert_bitcast_fusion), channel_id=1, replica_groups=mesh['dp'=8,'fsdp'=4] {'fsdp'}, dimensions={0}, use_global_device_ids=true | all-gather | bytes 23040 | tf_op jit(solution)/shard_map/all_gather | solution.py:259
  29.7 151.4 %all-gather.5.cloned.1.call-done = bf16[768,6144]{1,0:T(8,128)(2,1)} async-done(((bf16[192,6144]{1,0:T(8,128)(2,1)}), bf16[768,6144]{1,0:T(8,128)(2,1)}) %all-gather.5.cloned.1.call-update) | async-done | bytes 9437200 | tf_op jit(solution)/shard_map/all_gather | solution.py:257
  217.1 5.5 convolution_add_fusion.2
  222.6 48.3 %all-gather.7.cloned.1.call-done = bf16[3072,768]{1,0:T(8,128)(2,1)} async-done(((bf16[768,768]{1,0:T(8,128)(2,1)}), bf16[3072,768]{1,0:T(8,128)(2,1)}) %all-gather.7.cloned.1.call-update) | async-done | bytes 4718608 | tf_op jit(solution)/shard_map/all_gather | solution.py:258
  270.9 6.2 fusion.141
  278.2 4.0 convolution_add_fusion.3
  287.8 53.1 %all-gather.9.cloned.1.call-done = bf16[1024,768]{1,0:T(8,128)(2,1)} async-done(((bf16[32,768]{1,0:T(8,128)(2,1)}), bf16[1024,768]{1,0:T(8,128)(2,1)}) %all-gather.9.cloned.1.call-update) | async-done | bytes 1572880 | tf_op jit(solution)/shard_map/all_gather | solution.py:269
  348.2 99.0 %reduce-scatter.7.cloned.1.call-done = f32[32,768]{1,0:T(8,128)} async-done(((f32[1024,768]{1,0:T(8,128)}), f32[32,768]{1,0:T(8,128)}) %reduce-scatter.7.cloned.1.call-update) | async-done | bytes 98320 | tf_op jit(solution)/shard_map/reduce_scatter | solution.py:275
  450.0 4.3 fusion.124
  455.1 3.9 add_convert_fusion
  459.1 6.3 convert_reduce_fusion
  465.5 6.7 convert_reduce_fusion.1
  534.3 5.3 fusion.122
  539.6 9.6 %fusion = bf16[768,6144]{1,0:T(8,128)(2,1)} fusion(f32[768,3072]{1,0:T(8,128)} %fusion.122, f32[768,768]{1,0:T(8,128)S(1)} %fusion.146, f32[768,2304]{1,0:T(8,128)S(1)} %fusion.114, f32[768,3072]{1,0:T(8,128)S(1)} %fusion.123, f32[768,768]{1,0:T(8,128)} %fusion.147, f32[768,2304]{1,0:T(8,128)S(1)} %fusion.117), kind=kLoop, calls=%fused_computation.1 | loop fusion | flops 28311552 | bytes 47185920 | tf_op jit(solution)/shard_map/convert_element_type | solution.py:305
  550.8 3.6 fusion.27
  554.4 4.0 fusion.66
  560.3 149.7 %reduce-scatter.9.cloned.1.call-done = bf16[192,6144]{1,0:T(8,128)(2,1)} async-done(((bf16[768,6144]{1,0:T(8,128)(2,1)}), bf16[192,6144]{1,0:T(8,128)(2,1)}) %reduce-scatter.9.cloned.1.call-update) | async-done | bytes 2359312 | tf_op jit(solution)/shard_map/reduce_scatter | solution.py:304
  714.3 18.7 %reduce-scatter.13.cloned.1.call-done = bf16[192,12]{1,0:T(8,128)(2,1)} async-done(((bf16[768,12]{1,0:T(8,128)(2,1)}), bf16[192,12]{1,0:T(8,128)(2,1)}) %reduce-scatter.13.cloned.1.call-update) | async-done | bytes 4624
  733.9 12.3 %psum.23 = bf16[12,192]{1,0:T(8,128)(2,1)S(1)} all-reduce(bf16[12,192]{1,0:T(8,128)(2,1)S(1)} %copy.118), channel_id=1, replica_groups=mesh['dp'=8,'fsdp'=4] {'dp'}, use_global_device_ids=true, to_apply=%region_54.55 | all-reduce | flops 2304 | bytes 9216 | tf_op jit(solution)/shard_map/psum | solution.py:317
  747.5 61.5 %all-reduce.3.cloned.1.call-done = (bf16[192,6144]{1,0:T(8,128)(2,1)}, bf16[768,768]{1,0:T(8,128)(2,1)}) async-done(((bf16[192,6144]{1,0:T(8,128)(2,1)}, bf16[768,768]{1,0:T(8,128)(2,1)}), (bf16[192,6144]{1,0:T(8,128)(2,1)}, bf16[768,768]{1,0:T(8,128)(2,1)})) %all-reduce.3.cloned.1.call-update) | async-done | bytes 3538960 | tf_op jit(solution)/shard_map/psum | solution.py:315
  809.1 5.3 fusion.127
  816.5 7.3 fusion.129
  823.8 6.9 add_multiply_fusion
  (430 shorter events, 129.6 us)
Async XLA Ops:
  7.2 333.8 %copy-start = (bf16[32,768]{1,0:T(8,128)(2,1)S(1)}, bf16[32,768]{1,0:T(8,128)(2,1)}, u32[]{:S(2)}) copy-start(bf16[32,768]{1,0:T(8,128)(2,1)} %param.15) | copy-start | bytes 147460
  7.2 173.9 %all-gather.5.cloned.1.call-start = ((), (), s32[]{:S(2)}) async-start(), calls=%async_computation.4 | async-start | bytes 11796480 | tf_op jit(solution)/shard_map/all_gather | solution.py:257
  11.5 259.4 %all-gather.7.cloned.1.call-start = ((), (), s32[]{:S(2)}) async-start(), calls=%async_computation.5 | async-start | bytes 5898240 | tf_op jit(solution)/shard_map/all_gather | solution.py:258
  12.7 328.2 %all-gather.9.cloned.1.call-start = ((), (), s32[]{:S(2)}) async-start(), calls=%async_computation.6 | async-start | bytes 1622016 | tf_op jit(solution)/shard_map/all_gather | solution.py:269
  28.0 161.2 %copy-start.59 = (f32[768]{0:T(1024)}, f32[768]{0:T(1024)S(1)}, u32[]{:S(2)}) copy-start(f32[768]{0:T(1024)S(1)} %get-tuple-element.43) | copy-start | bytes 9220
  28.0 161.2 %copy-start.65 = (f32[768]{0:T(1024)}, f32[768]{0:T(1024)S(1)}, u32[]{:S(2)}) copy-start(f32[768]{0:T(1024)S(1)} %get-tuple-element.42) | copy-start | bytes 9220
  28.0 250.2 %copy-start.61 = (f32[768]{0:T(1024)}, f32[768]{0:T(1024)S(1)}, u32[]{:S(2)}) copy-start(f32[768]{0:T(1024)S(1)} %get-tuple-element.36) | copy-start | bytes 9220
  28.0 250.2 %copy-start.63 = (f32[768]{0:T(1024)}, f32[768]{0:T(1024)S(1)}, u32[]{:S(2)}) copy-start(f32[768]{0:T(1024)S(1)} %get-tuple-element.38) | copy-start | bytes 9220
  28.0 153.1 %copy-start.76 = (f32[256]{0:T(256)}, f32[256]{0:T(256)S(1)}, u32[]{:S(2)}) copy-start(f32[256]{0:T(256)S(1)} %get-tuple-element.112) | copy-start | bytes 3076
  28.0 161.1 %copy-start.78 = (f32[256]{0:T(256)}, f32[256]{0:T(256)S(1)}, u32[]{:S(2)}) copy-start(f32[256]{0:T(256)S(1)} %get-tuple-element.113) | copy-start | bytes 3076
  28.5 160.6 %copy-start.82 = (f32[256]{0:T(256)}, f32[256]{0:T(256)S(1)}, u32[]{:S(2)}) copy-start(f32[256]{0:T(256)S(1)} %fusion.108) | copy-start | bytes 3076
  28.5 152.6 %copy-start.80 = (f32[256]{0:T(256)}, f32[256]{0:T(256)S(1)}, u32[]{:S(2)}) copy-start(f32[256]{0:T(256)S(1)} %fusion.110) | copy-start | bytes 3076
  29.0 249.0 %copy-start.98 = (f32[16]{0:T(128)}, f32[16]{0:T(128)S(1)}, u32[]{:S(2)}) copy-start(f32[16]{0:T(128)S(1)} %get-tuple-element.85) | copy-start | bytes 196
  29.7 247.4 %copy-start.70 = (f32[16,16]{1,0:T(8,128)}, f32[16,16]{1,0:T(8,128)S(1)}, u32[]{:S(2)}) copy-start(f32[16,16]{1,0:T(8,128)S(1)} %get-tuple-element.115) | copy-start | bytes 3076
  199.7 314.3 %copy-start.33 = (f32[16,12,16]{2,1,0:T(8,128)}, f32[16,12,16]{2,1,0:T(8,128)S(1)}, u32[]{:S(2)}) copy-start(f32[16,12,16]{2,1,0:T(8,128)S(1)} %log_add_fusion.1) | copy-start | bytes 36868
  285.3 161.9 %copy-start.58 = (f32[16,768]{1,0:T(8,128)}, f32[16,768]{1,0:T(8,128)S(1)}, u32[]{:S(2)}) copy-start(f32[16,768]{1,0:T(8,128)S(1)} %multiply_reduce_fusion.7) | copy-start | bytes 147460
  287.3 159.9 %reduce-scatter.7.cloned.1.call-start = ((), (), s32[]{:S(2)}) async-start(), calls=%async_computation.7 | async-start | bytes 3244032 | tf_op jit(solution)/shard_map/reduce_scatter | solution.py:275
  346.3 214.0 %reduce-scatter.11.cloned.1.call-start = ((), (), s32[]{:S(2)}) async-start(), calls=%async_computation.9 | async-start | bytes 5898240 | tf_op jit(solution)/shard_map/reduce_scatter | solution.py:307
  459.0 251.0 %reduce-scatter.9.cloned.1.call-start = ((), (), s32[]{:S(2)}) async-start(), calls=%async_computation.8 | async-start | bytes 11796480 | tf_op jit(solution)/shard_map/reduce_scatter | solution.py:304
  549.3 183.8 %reduce-scatter.13.cloned.1.call-start = ((), (), s32[]{:S(2)}) async-start(), calls=%async_computation.10 | async-start | bytes 245760
  559.2 153.0 %copy-start.11 = (f32[256,768]{1,0:T(8,128)S(1)}, f32[256,768]{1,0:T(8,128)}, u32[]{:S(2)}) copy-start(f32[256,768]{1,0:T(8,128)} %copy-done.10) | copy-start | bytes 2359300
  559.2 153.0 %copy-start.104 = (f32[256]{0:T(256)S(1)}, f32[256]{0:T(256)}, u32[]{:S(2)}) copy-start(f32[256]{0:T(256)} %copy-done.103) | copy-start | bytes 3076
  560.3 248.8 %all-reduce.3.cloned.1.call-start = ((), (), s32[]{:S(2)}) async-start(), calls=%async_computation.11 | async-start | bytes 7077888 | tf_op jit(solution)/shard_map/psum | solution.py:315
  712.7 103.8 %slice-start = ((s8[4718592]{0:T(1024)(128)(4,1)}), s8[524288]{0:T(1024)(128)(4,1)S(1)}, s32[]{:S(2)}) async-start(s8[4718592]{0:T(1024)(128)(4,1)} %bitcast.87), calls=%async_computation.12 | async-start | bytes 1048576
  (111 other events, 797.3 us)
Sparse Core Ops, SparseCore 0:
  11.6 169.4 all-gather.4
  183.3 87.5 all-gather.6
  287.4 53.4 all-gather.8
  346.8 100.3 reduce-scatter.6
  459.1 84.2 reduce-scatter.10
  549.4 160.5 reduce-scatter.8
  712.8 20.1 reduce-scatter.12
  736.9 72.1 all-reduce.2
where the time goes:
time: 846 us; the launch traced here: 838 us
  waiting for transfers between devices  582 us (69%)
  matrix products  101 us (12%)
  other arithmetic  57.4 us (7%)
  local copies, waits for them, and re-layouts  53.3 us (6%)
  blocking collectives  27.1 us (3%)
  between operations  16.6 us (2%)
    all_gather x1, waiting for transfers between devices, body(): lax.all_gather(own_copies[0], 'fsdp', axis=0, tiled=True)  151 us
    reduce_scatter x1, waiting for transfers between devices, body(): lax.psum_scatter(wide_sum.astype(jnp.bfloat16), 'fsdp', scatter_dimension...  150 us
    reduce_scatter x1, waiting for transfers between devices, body(): lax.psum_scatter(lax.dot_general(slopes, images, contract_rows, preferred...  99 us
    psum x1, waiting for transfers between devices, body(): lax.psum(shares[0].astype(jnp.bfloat16), 'dp').astype(jnp.float32)  61.5 us
    all_gather x1, waiting for transfers between devices, body(): all_texts = lax.all_gather(local_texts, ('dp', 'fsdp'), axis=0, tiled=True)  53.1 us
    all_gather x1, waiting for transfers between devices, body(): lax.all_gather(own_copies[1], 'fsdp', axis=0, tiled=True)  48.3 us
    unnamed x9, waiting for transfers between devices  18.9 us
  transfers between devices with their start and end apart: 8, of which 7 were waited for; matrix products, arithmetic and copies ran while one was open for 17% of the time, Pallas kernels for 0%

commit v1 on v0

v1 whole, which is shorter than its diff:
```python
import functools

import jax
import jax.numpy as jnp
from jax import lax
from jax.experimental import pallas as pl
from jax.experimental.pallas import tpu as pltpu
from jax.sharding import PartitionSpec as P

HEADS = 12
SEQ = 16
PIECE = 384
GROUP = 8

norm_epsilon = 1e-06
masked_score = -1e30
learn_rate = 0.02
momentum_decay = 0.5
average_decay = 0.5
gelu_scale = 0.7978845608028654
gelu_cube = 0.044715

f32 = jnp.float32
bf16 = jnp.bfloat16
VMEM = pl.BlockSpec(memory_space=pltpu.VMEM)
SMEM = pl.BlockSpec(memory_space=pltpu.SMEM)
ANY = pl.BlockSpec(memory_space=pl.ANY)
PARAMS = pltpu.CompilerParams(vmem_limit_bytes=50 * 1024 * 1024)


def dot(left, right):
    return lax.dot_general(left, right, (((1,), (0,)), ((), ())), preferred_element_type=f32)


def dot_nt(left, right):
    return lax.dot_general(left, right, (((1,), (1,)), ((), ())), preferred_element_type=f32)


def dot_tn(left, right):
    return lax.dot_general(left, right, (((0,), (0,)), ((), ())), preferred_element_type=f32)


def shape(dims, kind):
    return jax.ShapeDtypeStruct(dims, kind)


def cost(flops, moved):
    return pl.CostEstimate(flops=int(flops), bytes_accessed=int(moved), transcendentals=0)


def norm_parts(values):
    centre = values - jnp.mean(values, axis=-1, keepdims=True)
    inv = lax.rsqrt(jnp.mean(centre * centre, axis=-1, keepdims=True) + norm_epsilon)
    return centre * inv, inv


def norm_back(grad, scaled, inv, gain):
    d_scaled = grad * gain
    first = jnp.mean(d_scaled, axis=-1, keepdims=True)
    second = jnp.mean(d_scaled * scaled, axis=-1, keepdims=True)
    return inv * (d_scaled - first - scaled * second)


def piece_copies(info, fs, rows, sources, target, sems, is_down):
    copies = []
    for k in range(GROUP):
        for j in range(1, fs):
            shard = info[3 + j]
            place = info[3 + fs + k]
            low, high = (j - 1) * rows, j * rows
            for ref, first in sources[k]:
                start, end = max(low, first), min(high, first + ref.shape[0])
                if start >= end:
                    continue
                inner, count = start - low, end - start
                if is_down:
                    row = shard * (4 * rows) + (place % 4) * rows + inner
                    col = (place // 4) * PIECE
                else:
                    row = shard * rows + inner
                    col = place * PIECE
                copies.append(
                    pltpu.make_async_copy(
                        ref.at[pl.ds(start - first, count), :],
                        target.at[pl.ds(pl.multiple_of(row, 16), count), pl.ds(pl.multiple_of(col, 128), PIECE)],
                        sems.at[len(copies)],
                    )
                )
    return copies


def sources_of(refs):
    table = {}
    for core in range(2):
        own, over_x, over_y, diag_a, diag_b = refs[5 * core : 5 * core + 5]
        table[core] = [(own, 0)]
        table[2 + core] = [(over_x, 0)]
        table[4 + core] = [(over_y, 0)]
        table[6 + core] = [(diag_a, 0), (diag_b, diag_a.shape[0])]
    return table


def attend_forward(queries, keys, values, mask, half_low, half_high):
    both_q = jnp.concatenate([queries * half_low, queries * half_high], axis=0)
    scores = jnp.where(mask, dot_nt(both_q, keys) * 0.125, masked_score)
    top = jnp.max(scores, axis=-1, keepdims=True)
    raised = jnp.exp(scores - top)
    probs = raised / jnp.sum(raised, axis=-1, keepdims=True)
    return both_q, probs


def lane_halves():
    lane = lax.broadcasted_iota(jnp.int32, (1, 128), 1)
    low = (lane < 64).astype(f32)
    return low, low.astype(bf16), (1.0 - low).astype(bf16)


def caption_mask(valid_row):
    row = lax.broadcasted_iota(jnp.int32, (256, 128), 0)
    col = lax.broadcasted_iota(jnp.int32, (256, 128), 1)
    same = ((row & 127) // SEQ) == (col // SEQ)
    return same & (valid_row > 0.0)


def kernel_attention(fs, rows, info, hid, valid, vec, own, *rest):
    pieces, rest = rest[:10], rest[10:]
    qkv_ref, ctx_ref, h_ref, second_ref, w_out, w, own_buf, sems, own_sem, out_sem = rest
    tokens, width = hid.shape
    copies = piece_copies(info, fs, rows, sources_of(pieces), w, sems, False)
    for copy in copies:
        copy.start()
    own_copy = pltpu.make_async_copy(own.at[:, pl.ds(0, 4 * width)], own_buf, own_sem)
    own_copy.start()
    vecs = vec[...]
    scaled, _ = norm_parts(hid[...].astype(f32))
    normed = (scaled * vecs[0:1] + vecs[1:2]).astype(bf16)
    own_copy.wait()
    w[pl.ds(pl.multiple_of(info[0] * rows, 16), rows), :] = own_buf[...].astype(bf16)
    for copy in copies:
        copy.wait()
    out_copy = pltpu.make_async_copy(w, w_out, out_sem)
    out_copy.start()
    for part in range(3):
        cols = pl.ds(part * width, width)
        value = dot(normed, w[:, cols])
        if part == 0:
            value = value + vecs[2:3]
        if part == 2:
            value = value + vecs[3:4]
        qkv_ref[:, cols] = value.astype(bf16)
    low_f, low, high = lane_halves()

    def block(index, carry):
        at = pl.ds(pl.multiple_of(index * 128, 128), 128)
        mask = caption_mask(valid[:, at])
        for pair in range(width // 128):
            here = pair * 128
            queries = qkv_ref[at, here : here + 128]
            keys = qkv_ref[at, width + here : width + here + 128]
            values = qkv_ref[at, 2 * width + here : 2 * width + here + 128]
            _, probs = attend_forward(queries, keys, values, mask, low, high)
            context = dot(probs.astype(bf16), values)
            ctx_ref[at, here : here + 128] = jnp.where(low_f > 0.0, context[:128], context[128:]).astype(bf16)
        return carry

    lax.fori_loop(0, tokens // 128, block, 0)
    residual = hid[...].astype(f32) + (dot(ctx_ref[...], w[:, 3 * width :]) + vecs[4:5])
    h_ref[...] = residual
    scaled, _ = norm_parts(residual)
    second_ref[...] = (scaled * vecs[5:6] + vecs[6:7]).astype(bf16)
    out_copy.wait()


def kernel_up(fs, rows, info, second, bias, own, *rest):
    pieces, rest = rest[:10], rest[10:]
    u_ref, g_ref, w_out, w, own_buf, sems, own_sem, out_sem = rest
    width, hidden = w.shape
    copies = piece_copies(info, fs, rows, sources_of(pieces), w, sems, False)
    own_copy = pltpu.make_async_copy(own.at[:, pl.ds(4 * width, hidden)], own_buf, own_sem)
    own_copy.start()
    for copy in copies:
        copy.start()
    own_copy.wait()
    w[pl.ds(pl.multiple_of(info[0] * rows, 16), rows), :] = own_buf[...].astype(bf16)
    for copy in copies:
        copy.wait()
    out_copy = pltpu.make_async_copy(w, w_out, out_sem)
    out_copy.start()

    def block(index, carry):
        cols = pl.ds(pl.multiple_of(index * 512, 128), 512)
        value = dot(second[...], w[:, cols]) + bias[:, cols]
        u_ref[:, cols] = value
        inner = jnp.tanh(gelu_scale * (value + gelu_cube * value * value * value))
        g_ref[:, cols] = (0.5 * value * (1.0 + inner)).astype(bf16)
        return carry

    lax.fori_loop(0, hidden // 512, block, 0)
    out_copy.wait()


def kernel_down(fs, rows, info, g, h, vec, lens, keep, images, own, *rest):
    pieces, rest = rest[:10], rest[10:]
    out_ref, pooled_ref, inv_ref, logit_ref, stat_ref, w_out, w, own_buf, sems, own_sem, out_sem = rest
    tokens, width = h.shape
    captions = tokens // SEQ
    copies = piece_copies(info, fs, rows, sources_of(pieces), w, sems, True)
    own_copy = pltpu.make_async_copy(own, own_buf, own_sem)
    own_copy.start()
    for copy in copies:
        copy.start()
    own_copy.wait()
    w[pl.ds(pl.multiple_of(info[0] * 4 * rows, 16), 4 * rows), :] = own_buf[...].astype(bf16)
    for copy in copies:
        copy.wait()
    out_copy = pltpu.make_async_copy(w, w_out, out_sem)
    out_copy.start()
    block_rows = h[...] + (dot(g[...], w[...]) + vec[7:8, :])
    out_ref[...] = block_rows.astype(bf16)
    pooled = jnp.sum((block_rows * keep[...]).reshape(captions, SEQ, width), axis=1) / lens[...]
    inv = lax.rsqrt(jnp.sum(pooled * pooled, axis=-1, keepdims=True) + norm_epsilon)
    pooled_ref[...] = pooled
    inv_ref[...] = inv
    texts = (pooled * inv).astype(bf16)
    logits = dot_nt(texts, images[:, :width])
    logit_ref[...] = logits
    top = jnp.max(logits, axis=0, keepdims=True)
    stat_ref[0:1, :] = top
    stat_ref[1:2, :] = jnp.sum(jnp.exp(logits - top), axis=0, keepdims=True)
    out_copy.wait()


def put(info, half, place, value, mine, theirs):
    rows = value.shape[0]

    @pl.when(info[1] == half)
    def _():
        mine[place[0], pl.ds(place[1], rows), :] = value

    @pl.when(info[1] != half)
    def _():
        theirs[place[0], pl.ds(place[1], rows), :] = value


def kernel_loss(rows, info, logits, stats, labels, images, pooled, inv, lens, keep, g, dpl_ref, dy_ref, bias_ref, mine, theirs):
    captions, width = pooled.shape
    tokens, hidden = g.shape
    lse = stats[0:1, :] + jnp.log(stats[1:2, :])
    number = lax.broadcasted_iota(jnp.int32, logits.shape, 0) + info[2] * captions
    onehot = (labels[...] == number).astype(f32)
    slopes = (jnp.exp(logits[...] - lse) - onehot).astype(bf16)
    text_grad = dot(slopes, images[:, :width])
    pool, inv_v = pooled[...], inv[...]
    d_pooled = inv_v * text_grad - inv_v**3 * pool * jnp.sum(pool * text_grad, axis=-1, keepdims=True)
    dpl = d_pooled / lens[...]
    dpl_ref[...] = dpl
    d_out = jnp.broadcast_to(dpl[:, None, :], (captions, SEQ, width)).reshape(tokens, width) * keep[...]
    dy = d_out.astype(bf16)
    dy_ref[...] = dy
    bias_ref[...] = jnp.sum(dy.astype(f32), axis=0, keepdims=True)
    for part in range(hidden // width):
        grad = dot_tn(g[:, part * width : (part + 1) * width], dy).astype(bf16)
        for sub in range(width // rows):
            first = part * width + sub * rows
            shard, quarter = first // (4 * rows), (first % (4 * rows)) // rows
            for half in range(2):
                value = grad[sub * rows : (sub + 1) * rows, half * PIECE : (half + 1) * PIECE]
                put(info, half, (quarter, shard * rows), value, mine, theirs)


def kernel_up_back(info, dy, u, second, w_down, du_ref, bias_ref, mine, theirs):
    tokens, hidden = u.shape
    for part in range(hidden // 768):
        cols = slice(part * 768, (part + 1) * 768)
        d_gelu = dot_nt(dy[...], w_down[cols, :])
        value = u[:, cols]
        square = value * value
        inner = jnp.tanh(gelu_scale * (value + gelu_cube * value * square))
        slope = 0.5 * (1.0 + inner) + (0.5 * gelu_scale) * value * (1.0 - inner * inner) * (1.0 + (3.0 * gelu_cube) * square)
        du = (d_gelu * slope).astype(bf16)
        du_ref[:, cols] = du
        bias_ref[:, cols] = jnp.sum(du.astype(f32), axis=0, keepdims=True)
    turned = second[...].T
    for place in range(hidden // PIECE):
        grad = dot(turned, du_ref[:, place * PIECE : (place + 1) * PIECE]).astype(bf16)
        put(info, place // 4, (place % 4, 0), grad, mine, theirs)


def kernel_attention_back(info, dpl, keep, du, h, hid, qkv, ctx, valid, vec, w_up, w_att, dh_ref, dqkv_ref, grads_ref, mine, theirs):
    tokens, width = h.shape
    captions = tokens // SEQ
    vecs = vec[...]
    d_second = dot_nt(du[...], w_up[...])
    scaled, inv = norm_parts(h[...])
    d_out = jnp.broadcast_to(dpl[...][:, None, :], (captions, SEQ, width)).reshape(tokens, width) * keep[...]
    dh = d_out + norm_back(d_second, scaled, inv, vecs[5:6])
    dh_ref[...] = dh
    da = dh.astype(bf16)
    grads_ref[2:3, :] = jnp.sum(da.astype(f32), axis=0, keepdims=True)
    grads_ref[3:4, :] = jnp.sum(d_second * scaled, axis=0, keepdims=True)
    grads_ref[4:5, :] = jnp.sum(d_second, axis=0, keepdims=True)
    d_ctx = dot_nt(da, w_att[:, 3 * width :]).astype(bf16)
    dqkv_ref[:, :width] = d_ctx
    low_f, low, high = lane_halves()

    def block(index, carry):
        at = pl.ds(pl.multiple_of(index * 128, 128), 128)
        mask = caption_mask(valid[:, at])
        for pair in range(width // 128):
            here = pair * 128
            queries = qkv[at, here : here + 128]
            keys = qkv[at, width + here : width + here + 128]
            values = qkv[at, 2 * width + here : 2 * width + here + 128]
            both_q, probs = attend_forward(queries, keys, values, mask, low, high)
            d_context = dqkv_ref[at, here : here + 128]
            both_d = jnp.concatenate([d_context * low, d_context * high], axis=0)
            d_probs = dot_nt(both_d, values)
            weighted = probs * d_probs
            d_scores = (weighted - probs * jnp.sum(weighted, axis=-1, keepdims=True)).astype(bf16)
            d_both = dot(d_scores, keys) * 0.125
            d_queries = jnp.where(low_f > 0.0, d_both[:128], d_both[128:])
            d_keys = dot_tn(d_scores, both_q) * 0.125
            d_values = dot_tn(probs.astype(bf16), both_d)
            dqkv_ref[at, here : here + 128] = d_queries.astype(bf16)
            dqkv_ref[at, width + here : width + here + 128] = d_keys.astype(bf16)
            dqkv_ref[at, 2 * width + here : 2 * width + here + 128] = d_values.astype(bf16)
        return carry

    lax.fori_loop(0, tokens // 128, block, 0)
    grads_ref[0:1, :] = jnp.sum(dqkv_ref[:, :width].astype(f32), axis=0, keepdims=True)
    grads_ref[1:2, :] = jnp.sum(dqkv_ref[:, 2 * width :].astype(f32), axis=0, keepdims=True)
    scaled, _ = norm_parts(hid[...].astype(f32))
    normed = (scaled * vecs[0:1] + vecs[1:2]).astype(bf16)
    turned = normed.T
    for place in range(6):
        grad = dot(turned, dqkv_ref[:, place * PIECE : (place + 1) * PIECE]).astype(bf16)
        put(info, place // 4, (place % 4, 0), grad, mine, theirs)
    turned = ctx[...].T
    for place in range(6, 8):
        at = (place - 6) * PIECE
        grad = dot(turned, da[:, at : at + PIECE]).astype(bf16)
        put(info, place // 4, (place % 4, 0), grad, mine, theirs)


def kernel_input_back(dqkv, dh, hid, vec, w_att, out_ref, grads_ref):
    width = hid.shape[1]
    d_normed = dot_nt(dqkv[...], w_att[:, : 3 * width])
    scaled, inv = norm_parts(hid[...].astype(f32))
    out_ref[...] = dh[...] + norm_back(d_normed, scaled, inv, vec[0:1, :])
    grads_ref[0:1, :] = jnp.sum(d_normed * scaled, axis=0, keepdims=True)
    grads_ref[1:2, :] = jnp.sum(d_normed, axis=0, keepdims=True)


def renew_state(master, momentum, average, gradient):
    momentum_new = momentum_decay * momentum + gradient
    master_new = master - learn_rate * (gradient + momentum_decay * momentum_new)
    average_new = average_decay * average + (1.0 - average_decay) * master_new
    return (master_new, momentum_new, average_new, master_new.astype(bf16))


def kernel_renew(fs, info, grad_a, grad_b, master, momentum, average, *rest):
    outs = rest[-4:]
    step = pl.program_id(0)

    def write(grad):
        new = renew_state(master[...], momentum[...], average[...], grad[0].astype(f32))
        for ref, value in zip(outs, new):
            ref[...] = value

    @pl.when(step < 4)
    def _():
        write(grad_a)

    @pl.when(step >= 4)
    def _():
        write(grad_b)


def renew(info, fs, rows, grads, master, momentum, average, column, earlier):
    def place(step, info):
        rel = 2 * (step % 4) + step // 4
        spot = info[3 + fs + rel]
        if column is None:
            return (spot % 4, spot // 4)
        return (0, column + spot)

    block = pl.BlockSpec((rows, PIECE), place)
    in_specs = [
        pl.BlockSpec((1, rows, PIECE), lambda step, info: (jnp.minimum(step, 3), 0, 0)),
        pl.BlockSpec((1, rows, PIECE), lambda step, info: (jnp.maximum(step - 4, 0), 0, 0)),
        block,
        block,
        block,
    ]
    aliases = {}
    if earlier:
        in_specs += [ANY] * 4
        aliases = {6 + i: i for i in range(4)}
    kinds = [f32, f32, f32, bf16]
    return pl.pallas_call(
        functools.partial(kernel_renew, fs),
        grid_spec=pltpu.PrefetchScalarGridSpec(
            num_scalar_prefetch=1, grid=(GROUP,), in_specs=in_specs, out_specs=[block] * 4
        ),
        out_shape=[shape(master.shape, kind) for kind in kinds],
        input_output_aliases=aliases,
        compiler_params=PARAMS,
        cost_estimate=cost(0, rows * PIECE * GROUP * 28),
    )(info, grads[0], grads[1], master, momentum, average, *earlier)


def flip(count, bit):
    return [(i, i ^ bit) for i in range(count)]


def send(value, axis, count, bit):
    return lax.ppermute(value, axis, flip(count, bit))


def kernel_own(info, wide_a, wide_b, down, out_a, out_b, out_c):
    out_a[...] = wide_a[...].astype(bf16)
    out_b[...] = wide_b[...].astype(bf16)
    out_c[...] = down[...].astype(bf16)


def own_pieces(info, fs, rows, wide_master, down_master):
    def at(offset):
        return pl.BlockSpec((rows, PIECE), lambda step, info: (0, offset + info[3 + fs]))

    whole = pl.BlockSpec((rows, PIECE), lambda step, info: (0, 0))
    return pl.pallas_call(
        kernel_own,
        grid_spec=pltpu.PrefetchScalarGridSpec(
            num_scalar_prefetch=1,
            grid=(1,),
            in_specs=[
                at(0),
                at(GROUP),
                pl.BlockSpec((rows, PIECE), lambda step, info: (info[3 + fs] % 4, info[3 + fs] // 4)),
            ],
            out_specs=[whole] * 3,
        ),
        out_shape=[shape((rows, PIECE), bf16)] * 3,
        compiler_params=PARAMS,
    )(info, wide_master, wide_master, down_master)


def spread(piece, fs, dp):
    rows = piece.shape[0]
    near = jnp.concatenate([send(piece, "fsdp", fs, j) for j in range(1, fs)], axis=0)
    over_x = send(near, "dp", dp, 2)
    over_y = send(near, "dp", dp, 4)
    cut = (fs - 1) * rows // 32 * 16
    diag_a = send(over_x[:cut], "dp", dp, 4)
    diag_b = send(over_y[cut:], "dp", dp, 2)
    half = [near, over_x, over_y, diag_a, diag_b]
    return half + [send(value, "dp", dp, 1) for value in half]


def add(left, right):
    return (left.astype(f32) + right.astype(f32)).astype(bf16)


def pick(values, index, axis):
    return lax.dynamic_index_in_dim(values, index, axis, keepdims=False)


def reduce_pieces(mine, theirs, fs, dp, z, x, y):
    rows = mine.shape[1] // fs
    half = mine.shape[1] // 2
    total = add(mine, send(theirs, "dp", dp, 1)).reshape(2, 2, 2 * half, PIECE)
    upper, lower = total[:, :, :half], total[:, :, half:]
    upper = add(pick(upper, x, 1), send(pick(upper, 1 - x, 1), "dp", dp, 2))
    lower = add(pick(lower, y, 0), send(pick(lower, 1 - y, 0), "dp", dp, 4))
    upper = add(pick(upper, y, 0), send(pick(upper, 1 - y, 0), "dp", dp, 4))
    lower = add(pick(lower, x, 0), send(pick(lower, 1 - x, 0), "dp", dp, 2))
    own = jnp.concatenate([upper, lower], axis=0)
    bit = GROUP
    while bit < dp:
        own = add(own, send(own, "dp", dp, bit))
        bit *= 2
    own = own.reshape(fs, rows, PIECE)
    total = pick(own, z, 0).astype(f32)
    for j in range(1, fs):
        total = total + send(pick(own, z ^ j, 0), "fsdp", fs, j).astype(f32)
    return total.astype(bf16)


def share_pieces(piece, dp):
    rows = piece.shape[0]
    over_x = send(piece, "dp", dp, 2)
    over_y = send(piece, "dp", dp, 4)
    cut = rows // 32 * 16
    diag = jnp.concatenate([send(over_x[:cut], "dp", dp, 4), send(over_y[cut:], "dp", dp, 2)], axis=0)
    side = jnp.stack([piece, over_x, over_y, diag])
    return side, send(side, "dp", dp, 1)


def merge_stats(group):
    top = functools.reduce(jnp.maximum, [top for top, _ in group])
    return top, sum(mass * jnp.exp(old - top) for old, mass in group)


def exchange_stats(stats, fs, dp):
    def one_round(stats, hops):
        arrived = [stats] + [send(stats, axis, count, bit) for axis, count, bit in hops]
        top, mass = merge_stats([(a[0:1], a[1:2]) for a in arrived])
        return jnp.concatenate([top, mass], axis=0)

    stats = one_round(stats, [("dp", dp, 1)])
    stats = one_round(stats, [("fsdp", fs, j) for j in range(1, fs)])
    stats = one_round(stats, [("dp", dp, j) for j in range(2, dp, 2)])
    return stats


def body(
    fs,
    dp,
    hidden_in,
    lengths,
    images,
    labels,
    wide_master,
    down_master,
    vector_master,
    wide_momentum,
    down_momentum,
    vector_momentum,
    wide_average,
    down_average,
    vector_average,
):
    tokens, width = hidden_in.shape
    captions = lengths.shape[0]
    rows = wide_master.shape[0]
    hidden = wide_master.shape[1] - 4 * width
    rank, z = lax.axis_index("dp"), lax.axis_index("fsdp")
    core, x, y = rank % 2, rank // 2 % 2, rank // 4 % 2
    member = [rank ^ k for k in range(GROUP)]
    spots = [(m % 2) * 4 + (m // 4 % 2) * 2 + (m // 2 % 2) for m in member]
    info = jnp.stack([z, core, rank * fs + z] + [z ^ j for j in range(fs)] + spots).astype(jnp.int32)

    tags = jnp.stack([labels // 128, labels % 128], axis=1).astype(bf16)
    marked = jnp.concatenate([images, jnp.pad(tags, ((0, 0), (0, 126)))], axis=1)
    marked = lax.all_gather(marked, ("dp", "fsdp"), axis=0, tiled=True)
    total = marked.shape[0]
    all_labels = (marked[:, width].astype(jnp.int32) * 128 + marked[:, width + 1].astype(jnp.int32))[None, :]

    own_vec = vector_master.astype(bf16)
    shards = [own_vec] + [send(own_vec, "fsdp", fs, j) for j in range(1, fs)]
    slots = lax.broadcasted_iota(jnp.int32, (1, fs, 1), 1)
    vec = sum(jnp.where(slots == (z ^ j), shards[j].astype(f32)[:, None, :], 0.0) for j in range(fs))
    vec = jnp.pad(vec.reshape(12, width), ((0, 4), (0, 0)))
    up_bias = vec[8:12].reshape(1, hidden)

    place = jnp.arange(SEQ)
    keep = (place[None, :] < lengths[:, None]).astype(f32).reshape(tokens)
    valid, keep = keep[None, :], keep[:, None]
    lens = lengths.astype(f32)[:, None]

    piece_a, piece_b, piece_c = own_pieces(info, fs, rows, wide_master, down_master)
    parts_a = spread(piece_a, fs, dp)
    parts_b = spread(piece_b, fs, dp)
    parts_c = spread(piece_c, fs, dp)
    n_copies = GROUP * fs * 2
    scratch = [
        pltpu.SemaphoreType.DMA((n_copies,)),
        pltpu.SemaphoreType.DMA,
        pltpu.SemaphoreType.DMA,
    ]

    qkv, ctx, h, second, w_att = pl.pallas_call(
        functools.partial(kernel_attention, fs, rows),
        in_specs=[SMEM, VMEM, VMEM, VMEM, ANY] + [ANY] * 10,
        out_specs=[VMEM] * 4 + [ANY],
        out_shape=[
            shape((tokens, 3 * width), bf16),
            shape((tokens, width), bf16),
            shape((tokens, width), f32),
            shape((tokens, width), bf16),
            shape((width, 4 * width), bf16),
        ],
        scratch_shapes=[pltpu.VMEM((width, 4 * width), bf16), pltpu.VMEM((rows, 4 * width), f32)] + scratch,
        compiler_params=PARAMS,
        cost_estimate=cost(2 * tokens * width * width * 5, 16e6),
    )(info, hidden_in, valid, vec, wide_master, *parts_a)

    u, g, w_up = pl.pallas_call(
        functools.partial(kernel_up, fs, rows),
        in_specs=[SMEM, VMEM, VMEM, ANY] + [ANY] * 10,
        out_specs=[VMEM] * 2 + [ANY],
        out_shape=[
            shape((tokens, hidden), f32),
            shape((tokens, hidden), bf16),
            shape((width, hidden), bf16),
        ],
        scratch_shapes=[pltpu.VMEM((width, hidden), bf16), pltpu.VMEM((rows, hidden), f32)] + scratch,
        compiler_params=PARAMS,
        cost_estimate=cost(2 * tokens * width * hidden, 20e6),
    )(info, second, up_bias, wide_master, *parts_b)

    block_out, pooled, inv, logits, stats, w_down = pl.pallas_call(
        functools.partial(kernel_down, fs, rows),
        in_specs=[SMEM] + [VMEM] * 6 + [ANY] + [ANY] * 10,
        out_specs=[VMEM] * 5 + [ANY],
        out_shape=[
            shape((tokens, width), bf16),
            shape((captions, width), f32),
            shape((captions, 1), f32),
            shape((captions, total), f32),
            shape((2, total), f32),
            shape((hidden, width), bf16),
        ],
        scratch_shapes=[pltpu.VMEM((hidden, width), bf16), pltpu.VMEM(down_master.shape, f32)] + scratch,
        compiler_params=PARAMS,
        cost_estimate=cost(2 * tokens * width * hidden, 20e6),
    )(info, g, h, vec, lens, keep, marked, down_master, *parts_c)

    stats = exchange_stats(stats, fs, dp)

    halves = [shape((4, width, PIECE), bf16)] * 2
    dpl, dy, down_bias_grad, mine_c, theirs_c = pl.pallas_call(
        functools.partial(kernel_loss, rows),
        in_specs=[SMEM] + [VMEM] * 9,
        out_specs=[VMEM] * 5,
        out_shape=[shape((captions, width), f32), shape((tokens, width), bf16), shape((1, width), f32)] + halves,
        compiler_params=PARAMS,
        cost_estimate=cost(2 * tokens * width * hidden, 10e6),
    )(info, logits, stats, all_labels, marked, pooled, inv, lens, keep, g)
    grad_c = share_pieces(reduce_pieces(mine_c, theirs_c, fs, dp, z, x, y), dp)

    du, up_bias_grad, mine_b, theirs_b = pl.pallas_call(
        kernel_up_back,
        in_specs=[SMEM] + [VMEM] * 4,
        out_specs=[VMEM] * 4,
        out_shape=[shape((tokens, hidden), bf16), shape((1, hidden), f32)] + halves,
        compiler_params=PARAMS,
        cost_estimate=cost(4 * tokens * width * hidden, 20e6),
    )(info, dy, u, second, w_down)
    grad_b = share_pieces(reduce_pieces(mine_b, theirs_b, fs, dp, z, x, y), dp)

    dh, dqkv, some_grads, mine_a, theirs_a = pl.pallas_call(
        kernel_attention_back,
        in_specs=[SMEM] + [VMEM] * 11,
        out_specs=[VMEM] * 5,
        out_shape=[
            shape((tokens, width), f32),
            shape((tokens, 3 * width), bf16),
            shape((8, width), f32),
        ]
        + halves,
        compiler_params=PARAMS,
        cost_estimate=cost(2 * tokens * width * width * 12, 20e6),
    )(info, dpl, keep, du, h, hidden_in, qkv, ctx, valid, vec, w_up, w_att)
    grad_a = share_pieces(reduce_pieces(mine_a, theirs_a, fs, dp, z, x, y), dp)

    input_grad, norm_grads = pl.pallas_call(
        kernel_input_back,
        in_specs=[VMEM] * 5,
        out_specs=[VMEM] * 2,
        out_shape=[shape((tokens, width), f32), shape((2, width), f32)],
        compiler_params=PARAMS,
        cost_estimate=cost(2 * tokens * width * width * 3, 10e6),
    )(dqkv, dh, hidden_in, vec, w_att)

    vec_grad = jnp.concatenate(
        [norm_grads, some_grads[:5], down_bias_grad, up_bias_grad.reshape(4, width)], axis=0
    ).astype(bf16)
    bit = 1
    while bit < dp:
        vec_grad = add(vec_grad, send(vec_grad, "dp", dp, bit))
        bit *= 2
    vec_parts = vec_grad.reshape(12, fs, width // fs)
    vec_sum = pick(vec_parts, z, 1).astype(f32)
    for j in range(1, fs):
        vec_sum = vec_sum + send(pick(vec_parts, z ^ j, 1), "fsdp", fs, j).astype(f32)

    down_state = renew(info, fs, rows, grad_c, down_master, down_momentum, down_average, None, ())
    wide_state = renew(info, fs, rows, grad_b, wide_master, wide_momentum, wide_average, GROUP, ())
    wide_state = renew(info, fs, rows, grad_a, wide_master, wide_momentum, wide_average, 0, tuple(wide_state))
    vector_state = renew_state(vector_master, vector_momentum, vector_average, vec_sum)
    return (
        block_out,
        input_grad,
        wide_state[0],
        down_state[0],
        vector_state[0],
        wide_state[1],
        down_state[1],
        vector_state[1],
        wide_state[2],
        down_state[2],
        vector_state[2],
        wide_state[3],
        down_state[3],
        vector_state[3],
    )


def solution(mesh):
    tokens = P(("dp", "fsdp"), None)
    each = P(("dp", "fsdp"))
    by_row = P("fsdp", None)
    by_col = P(None, "fsdp")
    states = (by_row, by_row, by_col)
    return jax.shard_map(
        functools.partial(body, mesh.shape["fsdp"], mesh.shape["dp"]),
        mesh=mesh,
        in_specs=(tokens, each, tokens, each) + states * 3,
        out_specs=(tokens, tokens) + states * 4,
        check_vma=False,
    )
```

time: 846 us -> 411 us (0.49)
  waiting for transfers between devices: 582 us -> 110 us
  Pallas kernels: 0 us -> 132 us
  starting transfers between devices: 1.05 us -> 104 us
  matrix products: 101 us -> 0 us
  other arithmetic: 57.4 us -> 16.5 us
  blocking collectives: 27.1 us -> 0 us
  local copies, waits for them, and re-layouts: 53.3 us -> 28.2 us
    all_gather x3 -> x1, waiting for transfers between devices: 253 us -> 0.01 us  [body(): marked = lax.all_gather(marked, ('dp', 'fsdp'), axis=0, tiled=True)]
    reduce_scatter x3 -> x0, waiting for transfers between devices: 249 us -> none  [the longest x1 150 us: body(): lax.psum_scatter(wide_sum.astype(jnp.bfloat16), 'fsdp', scatter_dimension...]
    pallas_call x0 -> x11, Pallas kernels: none -> 132 us  [the longest x1 31.9 us: body(): pl.pallas_call(kernel_attention_back, in_specs=[SMEM] + [VMEM] * 11, out_...]
    ppermute x0 -> x91, waiting for transfers between devices: none -> 110 us  [send(): return lax.ppermute(value, axis, flip(count, bit))]
    ppermute x0 -> x91, starting transfers between devices: none -> 104 us  [send(): return lax.ppermute(value, axis, flip(count, bit))]
    dot_general x38 -> x0, matrix products: 101 us -> none  [the longest x2 13.1 us: backward(): lax.dot_general(d_branch, down_w, contract_cols, preferred_element_type=j...]
    psum x1 -> x0, waiting for transfers between devices: 61.5 us -> none  [body(): lax.psum(shares[0].astype(jnp.bfloat16), 'dp').astype(jnp.float32)]
    reshape x24 -> x2, local copies, waits for them, and re-layouts: 25.8 us -> 1.45 us  [the longest x1 1.44 us: body(): vec_parts = vec_grad.reshape(12, fs, width // fs)]
  transfers between devices with their start and end apart: 8 -> 92, of which waited for: 7 -> 42; matrix products, arithmetic and copies ran while one was open for 17% -> 7% of each run, Pallas kernels for 0% -> 13%
where the time goes in v1:
time: 411 us; the launch traced here: 406 us
  Pallas kernels  132 us (32%)
  waiting for transfers between devices  110 us (27%)
  starting transfers between devices  104 us (25%)
  local copies, waits for them, and re-layouts  28.2 us (7%)
  other arithmetic  16.5 us (4%)
  between operations  16 us (4%)
    ppermute x91, waiting for transfers between devices, send(): return lax.ppermute(value, axis, flip(count, bit))  110 us
    ppermute x91, starting transfers between devices, send(): return lax.ppermute(value, axis, flip(count, bit))  104 us
    pallas_call x1, Pallas kernels, body(): pl.pallas_call(kernel_attention_back, in_specs=[SMEM] + [VMEM] * 11, out_...  31.9 us
    pallas_call x3, Pallas kernels, renew(): pl.pallas_call(functools.partial(kernel_renew, fs), grid_spec=pltpu.Prefe...  27.6 us
    pallas_call x1, Pallas kernels, body(): pl.pallas_call(kernel_up_back, in_specs=[SMEM] + [VMEM] * 4, out_specs=[V...  17.2 us
    unnamed x63, local copies, waits for them, and re-layouts  15.1 us
    pallas_call x1, Pallas kernels, body(): pl.pallas_call(functools.partial(kernel_attention, fs, rows), in_specs=[S...  14.3 us
    pallas_call x1, Pallas kernels, body(): pl.pallas_call(functools.partial(kernel_up, fs, rows), in_specs=[SMEM, VM...  12.1 us
  transfers between devices with their start and end apart: 92, of which 42 were waited for; matrix products, arithmetic and copies ran while one was open for 7% of the time, Pallas kernels for 13%

profile of v1, /device:TPU:0, one launch (start us, length us, event | category | flops | bytes accessed | tf_op | source)
XLA Modules:
  0.0 406.0 jit_solution(5059327264812887881)
XLA Ops:
  20.1 3.5 collective-permute-start.16
  23.6 4.7 %collective-permute-start.17 = (bf16[192,384]{1,0:T(8,128)(2,1)S(1)}, bf16[192,384]{1,0:T(8,128)(2,1)S(1)}, u32[]{:S(2)}, u32[]{:S(2)}) collective-permute-start(bf16[192,384]{1,0:T(8,128)(2,1)S(1)} %get-tuple-element.61), channel_id=1, source_target_pairs={{0,3},{1,2},{2,1},{3,0},{4,7},{5,6},{6,5},{7,4},{8,11},{9,10},{10,... | collective-permute-start | bytes 442376 | tf_op jit(solution)/shard_map/ppermute | solution.py:417
  37.9 14.0 %collective-permute-done.16 = bf16[192,384]{1,0:T(8,128)(2,1)S(1)} collective-permute-done((bf16[192,384]{1,0:T(8,128)(2,1)S(1)}, bf16[192,384]{1,0:T(8,128)(2,1)S(1)}, u32[]{:S(2)}, u32[]{:S(2)}) %collective-permute-start.16) | collective-permute-done | bytes 147488 | tf_op jit(solution)/shard_map/ppermute | solution.py:417
  55.9 3.8 collective-permute-done.28
  74.1 5.0 %collective-permute-done.19.rest_2_ = bf16[576,384]{1,0:T(8,128)(2,1)S(1)} collective-permute-done((bf16[576,384]{1,0:T(8,128)(2,1)S(1)}, bf16[576,384]{1,0:T(8,128)(2,1)S(1)}, u32[]{:S(2)}, u32[]{:S(2)}) %collective-permute-start.19) | collective-permute-done | bytes 442400 | tf_op jit(solution)/shard_map/ppermute | solution.py:417
  107.5 14.3 %shard_map.237 = (bf16[512,2304]{1,0:T(8,128)(2,1)}, bf16[512,768]{1,0:T(8,128)(2,1)}, f32[512,768]{1,0:T(8,128)}, bf16[512,768]{1,0:T(8,128)(2,1)}, bf16[768,3072]{1,0:T(8,128)(2,1)}) custom-call(s32[15]{0:T(128)S(1)} %stack.117.info, bf16[512,768]{1,0:T(8,128)(2,1)} %hid.5, f32[1,512]{1,0:T(1,128)S(1)} %reshape.216.valid, f32[16,768]{1,0:T(8,128)S(1)} %pad.8.vec, ...), custom_call_target="tpu_custom_call" | custom-call | flops 3019898880 | bytes 16000000 | tf_op jit(solution)/shard_map/pallas_call | solution.py:572
  122.4 12.1 %shard_map.238 = (f32[512,3072]{1,0:T(8,128)}, bf16[512,3072]{1,0:T(8,128)(2,1)}, bf16[768,3072]{1,0:T(8,128)(2,1)}) custom-call(s32[15]{0:T(128)S(1)} %stack.117.info, bf16[512,768]{1,0:T(8,128)(2,1)} %get-tuple-element.60.second, f32[1,3072]{1,0:T(1,128)S(1)} %bitcast.153, f32[192,6144]{1,0:T(8,128)} %master.4, ...), custom_call_target="tpu_custom_call" | custom-call | flops 2415919104 | bytes 20000000 | tf_op jit(solution)/shard_map/pallas_call | solution.py:588
  144.1 10.4 %shard_map.239 = (bf16[512,768]{1,0:T(8,128)(2,1)}, f32[32,768]{1,0:T(8,128)S(1)}, f32[32,1]{1,0:T(8,128)S(1)}, f32[32,1024]{1,0:T(8,128)S(1)}, f32[2,1024]{1,0:T(2,128)S(1)}, /*index=5*/bf16[3072,768]{1,0:T(8,128)(2,1)}) custom-call(s32[15]{0:T(128)S(1)} %stack.117.info, bf16[512,3072]{1,0:T(8,128)(2,1)} %get-tuple-element.62.g, ...), custom_call_target="tpu_custom_call" | custom-call | flops 2415919104 | bytes 20000000 | tf_op jit(solution)/shard_map/pallas_call | solution.py:602
  169.9 9.9 %shard_map.240 = (f32[32,768]{1,0:T(8,128)S(1)}, bf16[512,768]{1,0:T(8,128)(2,1)S(1)}, f32[1,768]{1,0:T(1,128)S(1)}, bf16[4,768,384]{2,1,0:T(8,128)(2,1)}, bf16[4,768,384]{2,1,0:T(8,128)(2,1)}) custom-call(s32[15]{0:T(128)S(1)} %stack.117.info, f32[32,1024]{1,0:T(8,128)S(1)} %get-tuple-element.66.logits, f32[2,1024]{1,0:T(2,128)S(1)} %pad_maximum_fusion.9.stats, ...), custom_call_target="tpu_custom_call" | custom-call | flops 2415919104 | bytes 10000000 | tf_op jit(solution)/shard_map/pallas_call | solution.py:622
  179.8 17.2 %shard_map.241 = (bf16[512,3072]{1,0:T(8,128)(2,1)}, f32[1,3072]{1,0:T(1,128)S(1)}, bf16[4,768,384]{2,1,0:T(8,128)(2,1)S(1)}, bf16[4,768,384]{2,1,0:T(8,128)(2,1)}) custom-call(s32[15]{0:T(128)S(1)} %stack.117.info, bf16[512,768]{1,0:T(8,128)(2,1)S(1)} %get-tuple-element.71.dy, f32[512,3072]{1,0:T(8,128)} %get-tuple-element.72.u, ...), custom_call_target="tpu_custom_call" | custom-call | flops 4831838208 | bytes 20000000 | tf_op jit(solution)/shard_map/pallas_call | solution.py:632
  197.0 31.9 %shard_map.242 = (f32[512,768]{1,0:T(8,128)S(1)}, bf16[512,2304]{1,0:T(8,128)(2,1)}, f32[8,768]{1,0:T(8,128)S(1)}, bf16[4,768,384]{2,1,0:T(8,128)(2,1)}, bf16[4,768,384]{2,1,0:T(8,128)(2,1)}) custom-call(s32[15]{0:T(128)S(1)} %stack.117.info, f32[32,768]{1,0:T(8,128)S(1)} %get-tuple-element.70.dpl, f32[512,1]{1,0:T(8,128)S(1)} %reshape.234.keep, ...), custom_call_target="tpu_custom_call" | custom-call | flops 7247757312 | bytes 20000000 | tf_op jit(solution)/shard_map/pallas_call | solution.py:642
  229.4 6.8 %shard_map.243 = (f32[512,768]{1,0:T(8,128)}, f32[2,768]{1,0:T(2,128)S(1)}) custom-call(bf16[512,2304]{1,0:T(8,128)(2,1)} %get-tuple-element.79.dqkv, f32[512,768]{1,0:T(8,128)S(1)} %get-tuple-element.80.dh, bf16[512,768]{1,0:T(8,128)(2,1)S(1)} %copy-done.3, f32[16,768]{1,0:T(8,128)S(1)} %pad.8.vec, bf16[768,3072]{1,0:T(8,128)(2,1)} %get-tuple-element.78.w_att), custom_call_target="tpu_custom_call" | custom-call | flops 1811939328 | bytes 10000000 | tf_op jit(solution)/shard_map/pallas_call | solution.py:657
  254.1 6.2 %collective-permute-done.49 = bf16[2,384,384]{2,1,0:T(8,128)(2,1)S(1)} collective-permute-done((bf16[2,384,384]{2,1,0:T(8,128)(2,1)S(1)}, bf16[2,384,384]{2,1,0:T(8,128)(2,1)S(1)}, u32[]{:S(2)}, u32[]{:S(2)}) %collective-permute-start.49) | collective-permute-done | bytes 589856 | tf_op jit(solution)/shard_map/ppermute | solution.py:417
  262.1 10.9 %collective-permute-done.62 = bf16[2,384,384]{2,1,0:T(8,128)(2,1)S(1)} collective-permute-done((bf16[2,384,384]{2,1,0:T(8,128)(2,1)S(1)}, bf16[2,384,384]{2,1,0:T(8,128)(2,1)S(1)}, u32[]{:S(2)}, u32[]{:S(2)}) %collective-permute-start.62) | collective-permute-done | bytes 589856 | tf_op jit(solution)/shard_map/ppermute | solution.py:417
  277.4 8.3 %collective-permute-done.75 = bf16[2,384,384]{2,1,0:T(8,128)(2,1)S(1)} collective-permute-done((bf16[2,384,384]{2,1,0:T(8,128)(2,1)S(1)}, bf16[2,384,384]{2,1,0:T(8,128)(2,1)S(1)}, u32[]{:S(2)}, u32[]{:S(2)}) %collective-permute-start.75) | collective-permute-done | bytes 589856 | tf_op jit(solution)/shard_map/ppermute | solution.py:417
  291.1 4.5 %collective-permute-done.50 = bf16[384,384]{1,0:T(8,128)(2,1)S(1)} collective-permute-done((bf16[384,384]{1,0:T(8,128)(2,1)S(1)}, bf16[384,384]{1,0:T(8,128)(2,1)S(1)}, u32[]{:S(2)}, u32[]{:S(2)}) %collective-permute-start.50) | collective-permute-done | bytes 294944 | tf_op jit(solution)/shard_map/ppermute | solution.py:417
  310.7 5.9 %collective-permute-start.65 = (bf16[192,384]{1,0:T(8,128)(2,1)S(1)}, bf16[192,384]{1,0:T(8,128)(2,1)S(1)}, u32[]{:S(2)}, u32[]{:S(2)}) collective-permute-start(bf16[192,384]{1,0:T(8,128)(2,1)S(1)} %get-tuple-element.124), channel_id=1, source_target_pairs={{0,2},{1,3},{2,0},{3,1},{4,6},{5,7},{6,4},{7,5},{8,10},{9,11},{10,... | collective-permute-start | bytes 442376 | tf_op jit(solution)/shard_map/ppermute | solution.py:417
  316.6 7.7 %collective-permute-done.52 = bf16[192,384]{1,0:T(8,128)(2,1)S(1)} collective-permute-done((bf16[192,384]{1,0:T(8,128)(2,1)S(1)}, bf16[192,384]{1,0:T(8,128)(2,1)S(1)}, u32[]{:S(2)}, u32[]{:S(2)}) %collective-permute-start.52) | collective-permute-done | bytes 147488 | tf_op jit(solution)/shard_map/ppermute | solution.py:417
  331.9 3.3 collective-permute-done.64
  360.6 4.2 %collective-permute-done.90 = bf16[12,192]{1,0:T(8,128)(2,1)S(1)} collective-permute-done((bf16[12,192]{1,0:T(8,128)(2,1)S(1)}, bf16[12,192]{1,0:T(8,128)(2,1)S(1)}, u32[]{:S(2)}, u32[]{:S(2)}) %collective-permute-start.90) | collective-permute-done | bytes 4640 | tf_op jit(solution)/shard_map/ppermute | solution.py:417
  364.9 3.5 collective-permute-done.88
  371.1 9.4 %shard_map.244 = (f32[192,6144]{1,0:T(8,128)}, f32[192,6144]{1,0:T(8,128)}, f32[192,6144]{1,0:T(8,128)}, bf16[192,6144]{1,0:T(8,128)(2,1)}) custom-call(s32[15]{0:T(128)S(1)} %stack.117.info, bf16[4,192,384]{2,1,0:T(8,128)(2,1)S(1)} %pad_maximum_fusion.3.grad_a, bf16[4,192,384]{2,1,0:T(8,128)(2,1)S(1)} %collective-permute-done.71.grad_b, ...), custom_call_target="tpu_custom_call" | custom-call | bytes 16515072 | tf_op jit(solution)/shard_map/pallas_call | solution.py:400
  380.5 8.9 %shard_map.246 = (f32[768,768]{1,0:T(8,128)}, f32[768,768]{1,0:T(8,128)}, f32[768,768]{1,0:T(8,128)}, bf16[768,768]{1,0:T(8,128)(2,1)}) custom-call(s32[15]{0:T(128)S(1)} %stack.117.info, bf16[4,192,384]{2,1,0:T(8,128)(2,1)S(1)} %pad_maximum_fusion.5.grad_a, bf16[4,192,384]{2,1,0:T(8,128)(2,1)S(1)} %collective-permute-done.84.grad_b, ...), custom_call_target="tpu_custom_call" | custom-call | bytes 16515072 | tf_op jit(solution)/shard_map/pallas_call | solution.py:400
  389.4 9.3 %shard_map.245 = (f32[192,6144]{1,0:T(8,128)}, f32[192,6144]{1,0:T(8,128)}, f32[192,6144]{1,0:T(8,128)}, bf16[192,6144]{1,0:T(8,128)(2,1)}) custom-call(s32[15]{0:T(128)S(1)} %stack.117.info, bf16[4,192,384]{2,1,0:T(8,128)(2,1)S(1)} %pad_maximum_fusion.1.grad_a, ...), custom_call_target="tpu_custom_call", output_to_operand_aliasing={{0}: (6, {}), {1}: (7, {}), {2}: (8, {}), {3}: (9, {})} | custom-call | bytes 16515072 | tf_op jit(solution)/shard_map/pallas_call | solution.py:400
  (348 shorter events, 174.3 us)
Async XLA Ops:
  7.2 131.0 %all-gather.2.cloned.1.call-start = ((), (), s32[]{:S(2)}) async-start(), calls=%async_computation | async-start | bytes 1892352 | tf_op jit(solution)/shard_map/all_gather | solution.py:545
  20.1 31.8 %collective-permute-start.16 = (bf16[192,384]{1,0:T(8,128)(2,1)S(1)}, bf16[192,384]{1,0:T(8,128)(2,1)S(1)}, u32[]{:S(2)}, u32[]{:S(2)}) collective-permute-start(bf16[192,384]{1,0:T(8,128)(2,1)S(1)} %get-tuple-element.61), channel_id=1, source_target_pairs={{0,2},{1,3},{2,0},{3,1},{4,6},{5,7},{6,4},{7,5},{8,10},{9,11},{10,... | collective-permute-start | bytes 442376 | tf_op jit(solution)/shard_map/ppermute | solution.py:417
  23.6 29.9 %collective-permute-start.17 = (bf16[192,384]{1,0:T(8,128)(2,1)S(1)}, bf16[192,384]{1,0:T(8,128)(2,1)S(1)}, u32[]{:S(2)}, u32[]{:S(2)}) collective-permute-start(bf16[192,384]{1,0:T(8,128)(2,1)S(1)} %get-tuple-element.61), channel_id=1, source_target_pairs={{0,3},{1,2},{2,1},{3,0},{4,7},{5,6},{6,5},{7,4},{8,11},{9,10},{10,... | collective-permute-start | bytes 442376 | tf_op jit(solution)/shard_map/ppermute | solution.py:417
  31.1 24.2 %collective-permute-start.27 = (bf16[192,384]{1,0:T(8,128)(2,1)S(1)}, bf16[192,384]{1,0:T(8,128)(2,1)S(1)}, u32[]{:S(2)}, u32[]{:S(2)}) collective-permute-start(bf16[192,384]{1,0:T(8,128)(2,1)S(1)} %get-tuple-element.64), channel_id=1, source_target_pairs={{0,1},{1,0},{2,3},{3,2},{4,5},{5,4},{6,7},{7,6},{8,9},{9,8},{10,11... | collective-permute-start | bytes 442376 | tf_op jit(solution)/shard_map/ppermute | solution.py:417
  33.6 26.1 %collective-permute-start.28 = (bf16[192,384]{1,0:T(8,128)(2,1)S(1)}, bf16[192,384]{1,0:T(8,128)(2,1)S(1)}, u32[]{:S(2)}, u32[]{:S(2)}) collective-permute-start(bf16[192,384]{1,0:T(8,128)(2,1)S(1)} %get-tuple-element.64), channel_id=1, source_target_pairs={{0,2},{1,3},{2,0},{3,1},{4,6},{5,7},{6,4},{7,5},{8,10},{9,11},{10,... | collective-permute-start | bytes 442376 | tf_op jit(solution)/shard_map/ppermute | solution.py:417
  35.9 29.2 %collective-permute-start.29 = (bf16[192,384]{1,0:T(8,128)(2,1)S(1)}, bf16[192,384]{1,0:T(8,128)(2,1)S(1)}, u32[]{:S(2)}, u32[]{:S(2)}) collective-permute-start(bf16[192,384]{1,0:T(8,128)(2,1)S(1)} %get-tuple-element.64), channel_id=1, source_target_pairs={{0,3},{1,2},{2,1},{3,0},{4,7},{5,6},{6,5},{7,4},{8,11},{9,10},{10,... | collective-permute-start | bytes 442376 | tf_op jit(solution)/shard_map/ppermute | solution.py:417
  71.3 20.0 %collective-permute-start.22 = (bf16[576,384]{1,0:T(8,128)(2,1)S(1)}, bf16[576,384]{1,0:T(8,128)(2,1)S(1)}, u32[]{:S(2)}, u32[]{:S(2)}) collective-permute-start(bf16[576,384]{1,0:T(8,128)(2,1)S(1)} %constant_dynamic-update-slice_fusion.3.rest_0_), channel_id=1, source_target_pairs={{0,4},{4,0},{8,12},{12,8},{16,20},{20,16},{24,28},{28,24},{1,5},{5... | collective-permute-start | bytes 1327112 | tf_op jit(solution)/shard_map/ppermute | solution.py:417
  71.8 20.1 %collective-permute-start.31 = (bf16[576,384]{1,0:T(8,128)(2,1)S(1)}, bf16[576,384]{1,0:T(8,128)(2,1)S(1)}, u32[]{:S(2)}, u32[]{:S(2)}) collective-permute-start(bf16[576,384]{1,0:T(8,128)(2,1)S(1)} %constant_dynamic-update-slice_fusion.6.rest_0_), channel_id=1, source_target_pairs={{0,16},{4,20},{8,24},{12,28},{16,0},{20,4},{24,8},{28,12},{1,17},{... | collective-permute-start | bytes 1327112 | tf_op jit(solution)/shard_map/ppermute | solution.py:417
  103.3 31.2 %collective-permute-start.34 = (bf16[576,384]{1,0:T(8,128)(2,1)S(1)}, bf16[576,384]{1,0:T(8,128)(2,1)S(1)}, u32[]{:S(2)}, u32[]{:S(2)}) collective-permute-start(bf16[576,384]{1,0:T(8,128)(2,1)S(1)} %constant_dynamic-update-slice_fusion.6.rest_0_), channel_id=1, source_target_pairs={{0,4},{4,0},{8,12},{12,8},{16,20},{20,16},{24,28},{28,24},{1,5},{5... | collective-permute-start | bytes 1327112 | tf_op jit(solution)/shard_map/ppermute | solution.py:417
  104.4 30.9 %collective-permute-start.35 = (bf16[576,384]{1,0:T(8,128)(2,1)S(1)}, bf16[576,384]{1,0:T(8,128)(2,1)S(1)}, u32[]{:S(2)}, u32[]{:S(2)}) collective-permute-start(bf16[576,384]{1,0:T(8,128)(2,1)S(1)} %collective-permute-done.30.rest_1_), channel_id=1, source_target_pairs={{0,4},{4,0},{8,12},{12,8},{16,20},{20,16},{24,28},{28,24},{1,5},{5... | collective-permute-start | bytes 1327112 | tf_op jit(solution)/shard_map/ppermute | solution.py:417
  104.7 31.3 %collective-permute-start.36 = (bf16[576,384]{1,0:T(8,128)(2,1)S(1)}, bf16[576,384]{1,0:T(8,128)(2,1)S(1)}, u32[]{:S(2)}, u32[]{:S(2)}) collective-permute-start(bf16[576,384]{1,0:T(8,128)(2,1)S(1)} %collective-permute-done.31.rest_2_), channel_id=1, source_target_pairs={{0,4},{4,0},{8,12},{12,8},{16,20},{20,16},{24,28},{28,24},{1,5},{5... | collective-permute-start | bytes 1327112 | tf_op jit(solution)/shard_map/ppermute | solution.py:417
  229.4 21.1 %collective-permute-start.72 = (bf16[4,768,384]{2,1,0:T(8,128)(2,1)}, bf16[4,768,384]{2,1,0:T(8,128)(2,1)}, u32[]{:S(2)}, u32[]{:S(2)}) collective-permute-start(bf16[4,768,384]{2,1,0:T(8,128)(2,1)} %get-tuple-element.92), channel_id=1, source_target_pairs={{0,4},{4,0},{8,12},{12,8},{16,20},{20,16},{24,28},{28,24},{1,5},{5... | collective-permute-start | bytes 7077896 | tf_op jit(solution)/shard_map/ppermute | solution.py:417
  240.2 104.5 %collective-permute-start.86 = (bf16[12,768]{1,0:T(8,128)(2,1)S(1)}, bf16[12,768]{1,0:T(8,128)(2,1)S(1)}, u32[]{:S(2)}, u32[]{:S(2)}) collective-permute-start(bf16[12,768]{1,0:T(8,128)(2,1)S(1)} %add_convert_fusion.5), channel_id=1, source_target_pairs={{0,8},{4,12},{8,0},{12,4},{16,24},{20,28},{24,16},{28,20},{1,9},{5... | collective-permute-start | bytes 55304 | tf_op jit(solution)/shard_map/ppermute | solution.py:417
  245.8 28.9 %collective-permute-start.47 = (bf16[2,384,384]{2,1,0:T(8,128)(2,1)S(1)}, bf16[2,384,384]{2,1,0:T(8,128)(2,1)S(1)}, u32[]{:S(2)}, u32[]{:S(2)}) collective-permute-start(bf16[2,384,384]{2,1,0:T(8,128)(2,1)S(1)} %dynamic-slice_bitcast_fusion.5), channel_id=1, source_target_pairs={{0,8},{4,12},{8,0},{12,4},{16,24},{20,28},{24,16},{28,20},{1,9},{5... | collective-permute-start | bytes 1769480 | tf_op jit(solution)/shard_map/ppermute | solution.py:417
  249.9 23.1 %collective-permute-start.62 = (bf16[2,384,384]{2,1,0:T(8,128)(2,1)S(1)}, bf16[2,384,384]{2,1,0:T(8,128)(2,1)S(1)}, u32[]{:S(2)}, u32[]{:S(2)}) collective-permute-start(bf16[2,384,384]{2,1,0:T(8,128)(2,1)S(1)} %dynamic-slice_bitcast_fusion.2), channel_id=1, source_target_pairs={{0,16},{4,20},{8,24},{12,28},{16,0},{20,4},{24,8},{28,12},{1,17},{... | collective-permute-start | bytes 1769480 | tf_op jit(solution)/shard_map/ppermute | solution.py:417
  250.5 25.1 %collective-permute-start.60 = (bf16[2,384,384]{2,1,0:T(8,128)(2,1)S(1)}, bf16[2,384,384]{2,1,0:T(8,128)(2,1)S(1)}, u32[]{:S(2)}, u32[]{:S(2)}) collective-permute-start(bf16[2,384,384]{2,1,0:T(8,128)(2,1)S(1)} %dynamic-slice_bitcast_fusion.3), channel_id=1, source_target_pairs={{0,8},{4,12},{8,0},{12,4},{16,24},{20,28},{24,16},{28,20},{1,9},{5... | collective-permute-start | bytes 1769480 | tf_op jit(solution)/shard_map/ppermute | solution.py:417
  260.4 25.3 %collective-permute-start.75 = (bf16[2,384,384]{2,1,0:T(8,128)(2,1)S(1)}, bf16[2,384,384]{2,1,0:T(8,128)(2,1)S(1)}, u32[]{:S(2)}, u32[]{:S(2)}) collective-permute-start(bf16[2,384,384]{2,1,0:T(8,128)(2,1)S(1)} %dynamic-slice_bitcast_fusion), channel_id=1, source_target_pairs={{0,16},{4,20},{8,24},{12,28},{16,0},{20,4},{24,8},{28,12},{1,17},{... | collective-permute-start | bytes 1769480 | tf_op jit(solution)/shard_map/ppermute | solution.py:417
  274.7 20.9 %collective-permute-start.50 = (bf16[384,384]{1,0:T(8,128)(2,1)S(1)}, bf16[384,384]{1,0:T(8,128)(2,1)S(1)}, u32[]{:S(2)}, u32[]{:S(2)}) collective-permute-start(bf16[384,384]{1,0:T(8,128)(2,1)S(1)} %dynamic-slice_bitcast_fusion.10), channel_id=1, source_target_pairs={{0,8},{4,12},{8,0},{12,4},{16,24},{20,28},{24,16},{28,20},{1,9},{5... | collective-permute-start | bytes 884744 | tf_op jit(solution)/shard_map/ppermute | solution.py:417
  275.6 21.6 %collective-permute-start.48 = (bf16[384,384]{1,0:T(8,128)(2,1)S(1)}, bf16[384,384]{1,0:T(8,128)(2,1)S(1)}, u32[]{:S(2)}, u32[]{:S(2)}) collective-permute-start(bf16[384,384]{1,0:T(8,128)(2,1)S(1)} %dynamic-slice_bitcast_fusion.11), channel_id=1, source_target_pairs={{0,16},{4,20},{8,24},{12,28},{16,0},{20,4},{24,8},{28,12},{1,17},{... | collective-permute-start | bytes 884744 | tf_op jit(solution)/shard_map/ppermute | solution.py:417
  303.8 20.5 %collective-permute-start.52 = (bf16[192,384]{1,0:T(8,128)(2,1)S(1)}, bf16[192,384]{1,0:T(8,128)(2,1)S(1)}, u32[]{:S(2)}, u32[]{:S(2)}) collective-permute-start(bf16[192,384]{1,0:T(8,128)(2,1)S(1)} %get-tuple-element.127), channel_id=1, source_target_pairs={{0,2},{1,3},{2,0},{3,1},{4,6},{5,7},{6,4},{7,5},{8,10},{9,11},{10,... | collective-permute-start | bytes 442376 | tf_op jit(solution)/shard_map/ppermute | solution.py:417
  306.9 20.2 %collective-permute-start.66 = (bf16[192,384]{1,0:T(8,128)(2,1)S(1)}, bf16[192,384]{1,0:T(8,128)(2,1)S(1)}, u32[]{:S(2)}, u32[]{:S(2)}) collective-permute-start(bf16[192,384]{1,0:T(8,128)(2,1)S(1)} %get-tuple-element.123), channel_id=1, source_target_pairs={{0,3},{1,2},{2,1},{3,0},{4,7},{5,6},{6,5},{7,4},{8,11},{9,10},{10,... | collective-permute-start | bytes 442376 | tf_op jit(solution)/shard_map/ppermute | solution.py:417
  310.7 20.0 %collective-permute-start.65 = (bf16[192,384]{1,0:T(8,128)(2,1)S(1)}, bf16[192,384]{1,0:T(8,128)(2,1)S(1)}, u32[]{:S(2)}, u32[]{:S(2)}) collective-permute-start(bf16[192,384]{1,0:T(8,128)(2,1)S(1)} %get-tuple-element.124), channel_id=1, source_target_pairs={{0,2},{1,3},{2,0},{3,1},{4,6},{5,7},{6,4},{7,5},{8,10},{9,11},{10,... | collective-permute-start | bytes 442376 | tf_op jit(solution)/shard_map/ppermute | solution.py:417
  352.9 36.5 %collective-permute-start.58 = (bf16[4,192,384]{2,1,0:T(8,128)(2,1)S(1)}, bf16[4,192,384]{2,1,0:T(8,128)(2,1)S(1)}, u32[]{:S(2)}, u32[]{:S(2)}) collective-permute-start(bf16[4,192,384]{2,1,0:T(8,128)(2,1)S(1)} %pad_maximum_fusion.1.grad_a), channel_id=1, source_target_pairs={{0,4},{4,0},{8,12},{12,8},{16,20},{20,16},{24,28},{28,24},{1,5},{5... | collective-permute-start | bytes 1769480 | tf_op jit(solution)/shard_map/ppermute | solution.py:417
  356.1 24.4 %collective-permute-start.84 = (bf16[4,192,384]{2,1,0:T(8,128)(2,1)S(1)}, bf16[4,192,384]{2,1,0:T(8,128)(2,1)S(1)}, u32[]{:S(2)}, u32[]{:S(2)}) collective-permute-start(bf16[4,192,384]{2,1,0:T(8,128)(2,1)S(1)} %pad_maximum_fusion.5.grad_a), channel_id=1, source_target_pairs={{0,4},{4,0},{8,12},{12,8},{16,20},{20,16},{24,28},{28,24},{1,5},{5... | collective-permute-start | bytes 1769480 | tf_op jit(solution)/shard_map/ppermute | solution.py:417
  (94 other events, 854.8 us)
Sparse Core Ops, SparseCore 0:
  10.8 69.0 all-gather.1
